TPU v7x, 32 devices: a whole 2x2x4 slice. The times are simulated.
32 devices in a mesh: src: 4 (over y, x), reg: 8 (over z, core).
Axes of the slice: x: 2, y: 2, z: 4, core: 2. Of those that a mesh axis runs over, the one named last changes fastest.
Arguments:
- displacement: float32 [3, 5, 512, 1024], P(None, None, 'src', 'reg'), may hold values from -0.06 to 0.06
- velocity: float32 [3, 5, 512, 1024], P(None, None, 'src', 'reg'), may hold values from -6 to 6
- modulus: float32 [5, 512, 1024], P(None, 'src', 'reg'), may hold values from 0.5 to 2
- density: float32 [5, 512, 1024], P(None, 'src', 'reg'), may hold values from 0.8 to 1.25
- traces: float32 [32, 512, 9, 128], P(('src', 'reg')), may hold values from -18 to 18
- record_row: int32 [32, 512], P(('src', 'reg')), may hold values from 0 to 127, as said below
Outputs:
- final_displacement: float32 [3, 5, 512, 1024], P(None, None, 'src', 'reg')
- final_velocity: float32 [3, 5, 512, 1024], P(None, None, 'src', 'reg')
Inputs may be any that keep to these rules, and one draw needn't show every extreme that they name: `record_row`: for every destination device d and step t, the entries of slots (d * 4 + t) * 4 + k, k < 4, taken over all segmenting buffers in order, form a permutation of 0 to 127.
All inputs are finite; a program needn't handle non-finite values.
Results may differ from a plain program's by a relative error of at most 0.000061.
Values sent between devices are 32-bit elements; how exact they have to be, the bound alone decides.
A program may use at most 128 MiB of HBM per device.

v0:
```python
import functools
import math

import jax
import jax.numpy as jnp
import ml_dtypes
import numpy as np
from jax import lax
from jax.experimental import pallas as pl
from jax.experimental.pallas import tpu as pltpu
from jax.sharding import PartitionSpec as P

STEPS = 4
DT = 0.02
ROWS = 8
MESH = pl.DeviceIdType.MESH
F32 = jnp.float32
BF16 = jnp.bfloat16


def gll_tables():
    inner_node = math.sqrt(3.0 / 7.0)
    nodes = np.array([-1.0, -inner_node, 0.0, inner_node, 1.0])
    weights = np.array([0.1, 49.0 / 90.0, 32.0 / 45.0, 49.0 / 90.0, 0.1])
    legendre = (35.0 * nodes**4 - 30.0 * nodes**2 + 3.0) / 8.0
    derivative = np.zeros((5, 5))
    for target in range(5):
        for source in range(5):
            if target != source:
                derivative[target, source] = legendre[target] / (
                    legendre[source] * (nodes[target] - nodes[source])
                )
    derivative[0, 0] = -5.0
    derivative[4, 4] = 5.0
    return derivative, weights


def periodic_weights(length):
    _, weights = gll_tables()
    return np.tile(np.array([2.0 * weights[0], weights[1], weights[2], weights[3]]), length // 4)


def line_tables(length, node_rows, columns):
    derivative, weights = gll_tables()
    elements = length // 4

    def node_at(node):
        if node < 0:
            return length + 16 + node
        return node

    gradient = np.zeros((node_rows, columns))
    selection = np.zeros((node_rows, columns))
    quadrature = np.zeros(columns)
    for element in range(-1, elements):
        for i in range(5):
            if element < 0:
                column = length + elements + i
            elif i < 4:
                column = 4 * element + i
            else:
                column = length + element
            for j in range(5):
                gradient[node_at(4 * element + j), column] = derivative[i, j]
            selection[node_at(4 * element + i), column] = 1.0
            quadrature[column] = weights[i]
    return gradient, gradient[:length].T.copy(), selection, quadrature


def halves(table):
    table = np.asarray(table, np.float32)
    high = table.astype(ml_dtypes.bfloat16)
    return high, (table - high.astype(np.float32)).astype(ml_dtypes.bfloat16)


def split(values):
    high = values.astype(BF16)
    return high, (values - high.astype(F32)).astype(BF16)


def dot(a, b):
    return jnp.dot(a, b, preferred_element_type=F32)


def dot_right(values, high, low):
    a, b = split(values)
    return dot(a, high) + (dot(b, high) + dot(a, low))


def dot_left(high, low, values):
    a, b = split(values)
    return dot(high, a) + (dot(high, b) + dot(low, a))


def kernel(
    n_src, n_reg, groups, comps, depth_nodes,
    disp, vel, mod, dens, traces, codes,
    ge_h, ge_l, be_h, be_l, gn_h, gn_l, bn_h, bn_l, sel_e, sel_n, wq_e, wq_n, ew, nw,
    d, v, sent, landed, halo_out, halo_in, mod_out, mod_in, coef_e, coef_n, coef_d, inv, inj,
    a2a_send, a2a_recv, halo_send, halo_recv,
):
    n = n_src * n_reg
    ny, nx = disp.shape[1:]
    nz = depth_nodes
    my_src, my_reg = lax.axis_index("src"), lax.axis_index("reg")
    me = my_src * n_reg + my_reg
    derivative, weights = gll_tables()
    dw = [float(w) for w in weights]
    barrier = pltpu.get_barrier_semaphore()

    def coords(index):
        return (index // n_reg, lax.rem(index, n_reg))

    def greet(j, carry):
        pl.semaphore_signal(
            barrier, inc=1, device_id=coords(lax.rem(me + j, n)), device_id_type=MESH
        )
        return carry

    lax.fori_loop(1, n, greet, 0)

    ways = (
        (my_src, lax.rem(my_reg + n_reg - 1, n_reg)),
        (my_src, lax.rem(my_reg + 1, n_reg)),
        (lax.rem(my_src + n_src - 1, n_src), my_reg),
        (lax.rem(my_src + 1, n_src), my_reg),
    )

    def halo_copy(t, way):
        return pltpu.make_async_remote_copy(
            halo_out.at[t, way], halo_in.at[t, way],
            halo_send.at[t, way], halo_recv.at[t, way],
            device_id=ways[way], device_id_type=MESH,
        )

    def mod_copy(way):
        return pltpu.make_async_remote_copy(
            mod_out.at[way], mod_in.at[way],
            halo_send.at[STEPS, way], halo_recv.at[STEPS, way],
            device_id=ways[way], device_id_type=MESH,
        )

    def pack(target, p, plane):
        turned = plane.T
        target[0, p] = turned[0:8]
        target[1, p] = turned[nx - 8 : nx]
        target[2, p] = plane[0:8]
        target[3, p] = plane[ny - 8 : ny]

    def group_copy(g, j):
        peer = lax.rem(me + j, n)
        planes = 10 if g == 0 else 9
        return pltpu.make_async_remote_copy(
            sent.at[g, pl.ds(0, planes), pl.ds(pl.multiple_of(peer * ROWS, ROWS), ROWS)],
            landed.at[g, pl.ds(0, planes), pl.ds(pl.multiple_of(me * ROWS, ROWS), ROWS)],
            a2a_send.at[g, j], a2a_recv.at[g, j],
            device_id=coords(peer), device_id_type=MESH,
        )

    def relayout(g):
        for c in range(9):
            x = traces[:, c, :].reshape(n, groups, ROWS, nx)
            sent[g, c] = x[:, g].reshape(n * ROWS, nx)
        if g == 0:
            sent[0, 9] = codes[...]

    def start_group(g):
        def go(j, carry):
            group_copy(g, j).start()
            return carry

        lax.fori_loop(1, n, go, 0)

    def own_group(g):
        mine = pl.ds(pl.multiple_of(me * ROWS, ROWS), ROWS)
        landed[g, :, mine] = sent[g, :, mine]

    def first_pack(p, carry):
        plane = disp[p] + DT * vel[p]
        d[p] = plane
        v[p] = vel[p]
        pack(halo_out.at[0], p, plane)
        return carry

    def mod_pack(p, carry):
        pack(mod_out, p, mod[p])
        return carry

    relayout(0)
    lax.fori_loop(0, nz, mod_pack, 0)
    lax.fori_loop(0, comps * nz, first_pack, 0)
    pl.semaphore_wait(barrier, n - 1)
    for way in range(4):
        mod_copy(way).start()
        halo_copy(0, way).start()
    start_group(0)
    for g in range(1, groups):
        relayout(g)
        start_group(g)
    for g in range(groups):
        own_group(g)

    inv_w = ew[...] * nw[...]
    for z in range(nz):
        inv[z] = DT / (0.125 * dens[z] * (inv_w * dw[z]))
        coef_d[z] = mod[z] * (inv_w * (0.5 * dw[z]))
    area = 0.25 * inv_w
    spring = 0.5 * mod[0]
    impedance = jnp.sqrt(dens[0] * mod[0])

    blank = jnp.zeros((nx - 16, ny), F32)

    def east_ext(plane, right, left):
        turned = jnp.concatenate([right, left, blank], axis=0).T
        return jnp.concatenate([plane, turned], axis=1)

    for way in range(4):
        mod_copy(way).wait_recv()
    for z in range(nz):
        a, b = split(east_ext(mod[z], mod_in[0, z], mod_in[1, z]))
        wide_nw = jnp.concatenate([nw[...]] * (wq_e.shape[1] // nx), axis=1)
        coef_e[z] = (dot(a, sel_e[...]) + dot(b, sel_e[...])) * (
            wide_nw * wq_e[...] * (0.5 * dw[z])
        )
        a, b = split(jnp.concatenate([mod[z], mod_in[2, z], mod_in[3, z]], axis=0))
        coef_n[z] = (dot(sel_n[...], a) + dot(sel_n[...], b)) * (
            wq_n[...] * ew[0:1, :] * (0.5 * dw[z])
        )

    for t in range(STEPS):
        g = t * groups // STEPS
        for way in range(4):
            halo_copy(t, way).wait_recv()
        if t * groups % STEPS == 0:
            def arrived(j, carry, g=g):
                group_copy(g, j).wait_recv()
                return carry

        def component(c, carry, t=t):
            first = c * nz
            ds = [d[first + z] for z in range(nz)]
            depth = []
            for i in range(nz):
                slope = ds[0] * float(derivative[i, 0])
                for j in range(1, nz):
                    slope = slope + ds[j] * float(derivative[i, j])
                depth.append(slope * coef_d[i])
            for z in range(nz):
                force = depth[0] * float(derivative[0, z])
                for i in range(1, nz):
                    force = force + depth[i] * float(derivative[i, z])
                p = first + z
                flux = dot_right(
                    east_ext(ds[z], halo_in[t, 0, p], halo_in[t, 1, p]), ge_h[...], ge_l[...]
                ) * coef_e[z]
                force = force + dot_right(flux, be_h[...], be_l[...])
                ext = jnp.concatenate([ds[z], halo_in[t, 2, p], halo_in[t, 3, p]], axis=0)
                flux = dot_left(gn_h[...], gn_l[...], ext) * coef_n[z]
                force = force + dot_left(bn_h[...], bn_l[...], flux)
                if z == 0:
                    force = force + area * (impedance * v[p] + spring * ds[0])
                v[p] = v[p] - force * inv[z]
            return carry

        lax.fori_loop(0, comps, component, 0)
        if t * groups % STEPS == 0:
            lax.fori_loop(1, n, arrived, 0)
            blocks = [
                landed[0, 9, k * nx : (k + 1) * nx].T for k in range(n * ROWS // nx)
            ]
            code = jnp.concatenate(blocks, axis=1)
            lane_group = g * (nx // groups)
            code = code[lane_group : lane_group + 1]
            row = lax.broadcasted_iota(jnp.int32, (ny, n * ROWS), 0).astype(F32)
            places = [
                jnp.where(code == row + float(step * ny), 1.0, 0.0).astype(BF16)
                for step in range(t, t + STEPS // groups)
            ]
            places = jnp.concatenate(places, axis=0)
            for c in range(9):
                a, b = split(landed[g, c])
                inj[c] = dot(places, a) + dot(places, b)
        at = pl.ds((t % (STEPS // groups)) * ny, ny)
        for c in range(comps):
            bottom = area * (
                inj[c, at] + impedance * inj[comps + c, at] + spring * inj[2 * comps + c, at]
            )
            v[c * nz] = v[c * nz] + bottom * inv[0]
        if t < STEPS - 1:

            def update(p, carry, t=t):
                plane = d[p] + DT * v[p]
                d[p] = plane
                pack(halo_out.at[t + 1], p, plane)
                return carry

            lax.fori_loop(0, comps * nz, update, 0)
            for way in range(4):
                halo_copy(t + 1, way).start()

    for way in range(4):
        mod_copy(way).wait_send()
        for t in range(STEPS):
            halo_copy(t, way).wait_send()
    for g in range(groups):

        def gone(j, carry, g=g):
            group_copy(g, j).wait_send()
            return carry

        lax.fori_loop(1, n, gone, 0)


def local(n_src, n_reg, displacement, velocity, modulus, density, traces, record_row):
    comps, nz, ny, nx = displacement.shape
    n = n_src * n_reg
    slots = traces.shape[1] // n
    per_step = slots // STEPS
    records = traces[0]
    code = (record_row[0].reshape(n, STEPS, per_step)
            + (jnp.arange(STEPS, dtype=jnp.int32) * ny)[None, :, None]).reshape(n, slots)
    groups = max(1, slots // ROWS)
    if slots != groups * ROWS or STEPS % groups:
        groups = 1
        pad = -slots % ROWS
        if slots + pad != ROWS:
            raise ValueError("slots")
        records = jnp.pad(records.reshape(n, slots, 9, nx), ((0, 0), (0, pad), (0, 0), (0, 0)))
        records = records.reshape(n * ROWS, 9, nx)
        code = jnp.pad(code, ((0, 0), (0, pad)), constant_values=-1)
    codes = code.reshape(n, groups, ROWS).transpose(0, 2, 1).reshape(n * ROWS, groups, 1)
    codes = jnp.broadcast_to(codes, (n * ROWS, groups, nx // groups)).reshape(n * ROWS, nx)
    codes = codes.astype(F32)

    wide = -(-(nx + nx // 4 + 5) // 128) * 128
    tall = -(-(ny + ny // 4 + 5) // 16) * 16
    ge, be, se, qe = line_tables(nx, 2 * nx, wide)
    gn, bn, sn, qn = line_tables(ny, ny + 16, tall)
    tables = [
        *halves(ge), *halves(be), *halves(gn.T), *halves(bn.T),
        se.astype(ml_dtypes.bfloat16), sn.T.astype(ml_dtypes.bfloat16),
        qe.astype(np.float32)[None, :],
        np.broadcast_to(qn.astype(np.float32)[:, None], (tall, nx)).copy(),
        np.broadcast_to(periodic_weights(nx).astype(np.float32)[None, :], (ny, nx)).copy(),
        np.broadcast_to(periodic_weights(ny).astype(np.float32)[:, None], (ny, nx)).copy(),
    ]
    planes = comps * nz
    args = [
        displacement.reshape(planes, ny, nx), velocity.reshape(planes, ny, nx),
        modulus, density, records, codes, *[jnp.asarray(table) for table in tables],
    ]
    vmem = pl.BlockSpec(memory_space=pltpu.VMEM)
    shape = jax.ShapeDtypeStruct((planes, ny, nx), F32)
    d, v = pl.pallas_call(
        functools.partial(kernel, n_src, n_reg, groups, comps, nz),
        out_shape=(shape, shape),
        in_specs=[vmem] * len(args),
        out_specs=(vmem, vmem),
        scratch_shapes=[
            pltpu.VMEM((groups, 10, n * ROWS, nx), F32),
            pltpu.VMEM((groups, 10, n * ROWS, nx), F32),
            pltpu.VMEM((STEPS, 4, planes, 8, nx), F32),
            pltpu.VMEM((STEPS, 4, planes, 8, nx), F32),
            pltpu.VMEM((4, nz, 8, nx), F32),
            pltpu.VMEM((4, nz, 8, nx), F32),
            pltpu.VMEM((nz, ny, wide), F32),
            pltpu.VMEM((nz, tall, nx), F32),
            pltpu.VMEM((nz, ny, nx), F32),
            pltpu.VMEM((nz, ny, nx), F32),
            pltpu.VMEM((9, STEPS // groups * ny, nx), F32),
            pltpu.SemaphoreType.DMA((groups, n)),
            pltpu.SemaphoreType.DMA((groups, n)),
            pltpu.SemaphoreType.DMA((STEPS + 1, 4)),
            pltpu.SemaphoreType.DMA((STEPS + 1, 4)),
        ],
        compiler_params=pltpu.CompilerParams(
            collective_id=0, has_side_effects=True, vmem_limit_bytes=56 * 1024 * 1024
        ),
    )(*args)
    return d.reshape(comps, nz, ny, nx), v.reshape(comps, nz, ny, nx)


def solution(mesh):
    in_specs = (
        P(None, None, "src", "reg"),
        P(None, None, "src", "reg"),
        P(None, "src", "reg"),
        P(None, "src", "reg"),
        P(("src", "reg"), None, None, None),
        P(("src", "reg"), None),
    )
    out_specs = (P(None, None, "src", "reg"), P(None, None, "src", "reg"))
    body = functools.partial(local, mesh.shape["src"], mesh.shape["reg"])
    return jax.shard_map(body, mesh=mesh, in_specs=in_specs, out_specs=out_specs, check_vma=False)
```

profile of v0, /device:TPU:16, one launch (start us, length us, event | category | flops | bytes accessed | tf_op | source)
XLA Modules:
  0.0 119.3 jit_solution(16228658025074323586)
XLA Ops:
  0.6 0.1 add.14
  0.7 0.1 add.15
  0.8 0.5 broadcast.18
  1.3 1.3 %reduce.3 = s32[512]{0:T(512)S(1)} reduce(s32[1,512]{1,0:T(1,128)} %param.25, s32[]{:T(128)} %broadcast.18), dimensions={0}, to_apply=%param.25.reduce_sub_computation.3 | reduce | bytes 4100 | tf_op args[5]
  2.7 0.1 reshape_squeeze.3
  2.8 0.1 convert_element_type.11
  2.9 0.8 copy.25.codes
  3.7 5.1 %copy.27 = f32[1,512,9,128]{3,2,1,0:T(8,128)} copy(f32[1,512,9,128]{3,1,2,0:T(8,128)} %param.24) | data formatting | bytes 4718592 | tf_op args[4]
  8.7 106.1 %shard_map.203 = (f32[15,128,128]{2,1,0:T(8,128)}, f32[15,128,128]{2,1,0:T(8,128)}) custom-call(f32[15,128,128]{2,1,0:T(8,128)} %bitcast.13, f32[15,128,128]{2,1,0:T(8,128)} %bitcast.14, f32[5,128,128]{2,1,0:T(8,128)} %mod.1, f32[5,128,128]{2,1,0:T(8,128)} %dens.1, f32[512,9,128]{2,1,0:T(8,128)} %bitcast.12, f32[256,128]{1,0:T(8,128)} %copy.25.codes, ...), custom_call_target="tpu_custom_call" | custom-call | tf_op jit(solution)/shard_map/pallas_call | solution.py:354
  114.9 2.2 %copy.30 = f32[3,5,128,128]{3,2,1,0:T(8,128)} copy(f32[3,5,128,128]{3,2,1,0:T(8,128)} %bitcast.16) | data formatting | bytes 1966080
  117.1 2.2 %copy.31 = f32[3,5,128,128]{3,2,1,0:T(8,128)} copy(f32[3,5,128,128]{3,2,1,0:T(8,128)} %bitcast.15) | data formatting | bytes 1966080
  (4 shorter events, 0.0 us)
where the time goes:
time: 120 us; the launch traced here: 119 us
  Pallas kernels  106 us (88%)
  local copies, waits for them, and re-layouts  11.2 us (9%)
  other arithmetic  1.37 us (1%)
    pallas_call x1, Pallas kernels, local(): pl.pallas_call(functools.partial(kernel, n_src, n_reg, groups, comps, nz)...  106 us
    unnamed x4, local copies, waits for them, and re-layouts  10.1 us

commit v1 on v0

--- a/solution.py
+++ b/solution.py
@@ -159,7 +159,7 @@
 
     def relayout(g):
         for c in range(9):
-            x = traces[:, c, :].reshape(n, groups, ROWS, nx)
+            x = traces[c].reshape(n, groups, ROWS, nx)
             sent[g, c] = x[:, g].reshape(n * ROWS, nx)
         if g == 0:
             sent[0, 9] = codes[...]
@@ -316,7 +316,7 @@
     n = n_src * n_reg
     slots = traces.shape[1] // n
     per_step = slots // STEPS
-    records = traces[0]
+    records = traces[0].transpose(1, 0, 2)
     code = (record_row[0].reshape(n, STEPS, per_step)
             + (jnp.arange(STEPS, dtype=jnp.int32) * ny)[None, :, None]).reshape(n, slots)
     groups = max(1, slots // ROWS)
@@ -325,8 +325,8 @@
         pad = -slots % ROWS
         if slots + pad != ROWS:
             raise ValueError("slots")
-        records = jnp.pad(records.reshape(n, slots, 9, nx), ((0, 0), (0, pad), (0, 0), (0, 0)))
-        records = records.reshape(n * ROWS, 9, nx)
+        records = jnp.pad(records.reshape(9, n, slots, nx), ((0, 0), (0, 0), (0, pad), (0, 0)))
+        records = records.reshape(9, n * ROWS, nx)
         code = jnp.pad(code, ((0, 0), (0, pad)), constant_values=-1)
     codes = code.reshape(n, groups, ROWS).transpose(0, 2, 1).reshape(n * ROWS, groups, 1)
     codes = jnp.broadcast_to(codes, (n * ROWS, groups, nx // groups)).reshape(n * ROWS, nx)

time: 120 us -> 113 us (0.942)
  local copies, waits for them, and re-layouts: 11.2 us -> 4.9 us
    unnamed x4 -> x5, local copies, waits for them, and re-layouts: 10.1 us -> 3.78 us
where the time goes in v1:
time: 113 us
  Pallas kernels  106 us (94%)
  local copies, waits for them, and re-layouts  4.9 us (4%)
  other arithmetic  1.37 us (1%)
    pallas_call x1, Pallas kernels, local(): pl.pallas_call(functools.partial(kernel, n_src, n_reg, groups, comps, nz)...  106 us
    unnamed x5, local copies, waits for them, and re-layouts  3.78 us

profile of v1, /device:TPU:16, one launch (start us, length us, event | category | flops | bytes accessed | tf_op | source)
XLA Modules:
  0.0 112.6 jit_solution(7193109590841253743)
XLA Ops:
  0.6 0.1 add.14
  0.7 0.1 add.15
  0.8 0.5 broadcast.18
  1.3 1.3 %reduce.3 = s32[512]{0:T(512)S(1)} reduce(s32[1,512]{1,0:T(1,128)} %param.25, s32[]{:T(128)} %broadcast.18), dimensions={0}, to_apply=%param.25.reduce_sub_computation.3 | reduce | bytes 4100 | tf_op args[5]
  2.7 0.1 reshape_squeeze.3
  2.8 0.1 convert_element_type.11
  2.9 0.8 copy.23.codes
  3.7 105.7 %shard_map.203 = (f32[15,128,128]{2,1,0:T(8,128)}, f32[15,128,128]{2,1,0:T(8,128)}) custom-call(f32[15,128,128]{2,1,0:T(8,128)} %bitcast.13, f32[15,128,128]{2,1,0:T(8,128)} %bitcast.14, f32[5,128,128]{2,1,0:T(8,128)} %mod.1, f32[5,128,128]{2,1,0:T(8,128)} %dens.1, f32[9,512,128]{2,1,0:T(8,128)} %bitcast.12, f32[256,128]{1,0:T(8,128)} %copy.23.codes, ...), custom_call_target="tpu_custom_call" | custom-call | tf_op jit(solution)/shard_map/pallas_call | solution.py:354
  109.3 0.0 copy-start
  109.3 2.3 %copy.26 = f32[3,5,128,128]{3,2,1,0:T(8,128)} copy(f32[3,5,128,128]{3,2,1,0:T(8,128)} %bitcast.16) | data formatting | bytes 1966080
  111.7 0.0 copy-done
  111.7 0.9 copy.27
  (4 shorter events, 0.0 us)
Async XLA Ops:
  109.3 2.3 %copy-start = (f32[15,128,128]{2,1,0:T(8,128)S(1)}, f32[15,128,128]{2,1,0:T(8,128)}, u32[]{:S(2)}) copy-start(f32[15,128,128]{2,1,0:T(8,128)} %get-tuple-element.5) | copy-start | bytes 2949124

commit v2 on v1

--- a/solution.py
+++ b/solution.py
@@ -162,7 +162,16 @@
             x = traces[c].reshape(n, groups, ROWS, nx)
             sent[g, c] = x[:, g].reshape(n * ROWS, nx)
         if g == 0:
-            sent[0, 9] = codes[...]
+            lane = lax.broadcasted_iota(jnp.int32, (n, ROWS, nx), 2)
+            turned = [
+                jnp.broadcast_to(codes[:, k * nx : (k + 1) * nx].astype(F32), (nx, nx)).T
+                for k in range(codes.shape[1] // nx)
+            ]
+            turned = jnp.concatenate(turned, axis=0).reshape(n, groups, ROWS, nx)
+            plane = turned[:, 0]
+            for k in range(1, groups):
+                plane = jnp.where(lane >= k * (nx // groups), turned[:, k], plane)
+            sent[0, 9] = plane.reshape(n * ROWS, nx)
 
     def start_group(g):
         def go(j, carry):
@@ -317,8 +326,8 @@
     slots = traces.shape[1] // n
     per_step = slots // STEPS
     records = traces[0].transpose(1, 0, 2)
-    code = (record_row[0].reshape(n, STEPS, per_step)
-            + (jnp.arange(STEPS, dtype=jnp.int32) * ny)[None, :, None]).reshape(n, slots)
+    step_of = np.arange(n * slots, dtype=np.int32) // per_step % STEPS
+    codes = record_row + jnp.asarray(step_of * ny)[None, :]
     groups = max(1, slots // ROWS)
     if slots != groups * ROWS or STEPS % groups:
         groups = 1
@@ -327,11 +336,8 @@
             raise ValueError("slots")
         records = jnp.pad(records.reshape(9, n, slots, nx), ((0, 0), (0, 0), (0, pad), (0, 0)))
         records = records.reshape(9, n * ROWS, nx)
-        code = jnp.pad(code, ((0, 0), (0, pad)), constant_values=-1)
-    codes = code.reshape(n, groups, ROWS).transpose(0, 2, 1).reshape(n * ROWS, groups, 1)
-    codes = jnp.broadcast_to(codes, (n * ROWS, groups, nx // groups)).reshape(n * ROWS, nx)
-    codes = codes.astype(F32)
-
+        codes = jnp.pad(codes.reshape(n, slots), ((0, 0), (0, pad)), constant_values=-1)
+        codes = codes.reshape(1, n * ROWS)
     wide = -(-(nx + nx // 4 + 5) // 128) * 128
     tall = -(-(ny + ny // 4 + 5) // 16) * 16
     ge, be, se, qe = line_tables(nx, 2 * nx, wide)

time: 113 us -> 111 us (0.982)
  local copies, waits for them, and re-layouts: 4.9 us -> 3.27 us
    unnamed x1 -> x0, other arithmetic: 1.34 us -> none
    add x0 -> x1, other arithmetic: none -> 1.28 us  [local(): codes = record_row + jnp.asarray(step_of * ny)[None, :]]
    unnamed x5 -> x4, local copies, waits for them, and re-layouts: 3.78 us -> 3.27 us
where the time goes in v2:
time: 111 us
  Pallas kernels  106 us (95%)
  local copies, waits for them, and re-layouts  3.27 us (3%)
  other arithmetic  1.28 us (1%)
    pallas_call x1, Pallas kernels, local(): pl.pallas_call(functools.partial(kernel, n_src, n_reg, groups, comps, nz)...  106 us
    unnamed x4, local copies, waits for them, and re-layouts  3.27 us

profile of v2, /device:TPU:16, one launch (start us, length us, event | category | flops | bytes accessed | tf_op | source)
XLA Modules:
  0.0 110.8 jit_solution(8296696578660582323)
XLA Ops:
  0.6 1.3 %add.3.codes = s32[1,512]{1,0:T(1,128)} add(s32[1,512]{1,0:T(1,128)} %param.26, s32[1,512]{1,0:T(1,128)} %constant.47) | non-fusion elementwise | flops 512 | bytes 6144 | tf_op jit(solution)/shard_map/add | solution.py:330
  1.9 105.6 %shard_map.212 = (f32[15,128,128]{2,1,0:T(8,128)}, f32[15,128,128]{2,1,0:T(8,128)}) custom-call(f32[15,128,128]{2,1,0:T(8,128)} %bitcast.8, f32[15,128,128]{2,1,0:T(8,128)} %bitcast.9, f32[5,128,128]{2,1,0:T(8,128)} %mod.1, f32[5,128,128]{2,1,0:T(8,128)} %dens.1, f32[9,512,128]{2,1,0:T(8,128)} %bitcast.7, s32[1,512]{1,0:T(1,128)} %add.3.codes, ...), custom_call_target="tpu_custom_call" | custom-call | tf_op jit(solution)/shard_map/pallas_call | solution.py:360
  107.6 0.0 copy-start
  107.6 2.3 %copy.25 = f32[3,5,128,128]{3,2,1,0:T(8,128)} copy(f32[3,5,128,128]{3,2,1,0:T(8,128)} %bitcast.11) | data formatting | bytes 1966080
  109.9 0.0 copy-done
  109.9 0.9 copy.26
Async XLA Ops:
  107.6 2.3 %copy-start = (f32[15,128,128]{2,1,0:T(8,128)S(1)}, f32[15,128,128]{2,1,0:T(8,128)}, u32[]{:S(2)}) copy-start(f32[15,128,128]{2,1,0:T(8,128)} %get-tuple-element.5) | copy-start | bytes 2949124
